TPU v7x, 32 devices: a whole 2x2x4 slice. The times are simulated.
32 devices in a mesh: rep: 16 (over z, x, core), exp: 2 (over y).
Axes of the slice: x: 2, y: 2, z: 4, core: 2. Of those that a mesh axis runs over, the one named last changes fastest.
Arguments:
- residual: bfloat16 [3, 64, 4096], P(None, ('rep', 'exp')), may hold values from -6 to 6
- queries: bfloat16 [3, 64, 4096], P(None, ('rep', 'exp')), may hold values from -30 to 30
- key_cache: bfloat16 [64, 1024, 256], P(('rep', 'exp')), may hold values from -6 to 6
- value_cache: bfloat16 [64, 1024, 256], P(('rep', 'exp')), may hold values from -6 to 6
- new_keys: bfloat16 [3, 64, 256], P(None, ('rep', 'exp')), may hold values from -6 to 6
- new_values: bfloat16 [3, 64, 256], P(None, ('rep', 'exp')), may hold values from -6 to 6
- cache_len: int32 [64], P(('rep', 'exp')), may hold values from 128 to 1024, as said below
- norm_gain: bfloat16 [4096], replicated, may hold values from 0.099609375 to 1.8984375
- expert_ids: int32 [3, 64, 8], P(None, ('rep', 'exp')), may hold values from 0 to 31, all different within a row; in each aligned block of 4 rows (0 to 3, 4 to 7, ..., all dimensions but the last counted through in order) at most 4 rows name the same one
- gate_scores: int32 [3, 64, 8], P(None, ('rep', 'exp')), may hold values from 1 to 1000
- gate_weight: bfloat16 [32, 1536, 4096], P('rep', 'exp'), may hold values from -0.09375 to 0.09375
- up_weight: bfloat16 [32, 1536, 4096], P('rep', 'exp'), may hold values from -0.09375 to 0.09375
- down_weight: bfloat16 [32, 1536, 4096], P('rep', 'exp'), may hold values from -0.15625 to 0.15625
Outputs:
- mixed: bfloat16 [3, 64, 4096], P(None, ('rep', 'exp'))
Inputs may be any that keep to these rules, and one draw needn't show every extreme that they name: `expert_ids`: within each step and each aligned block of 4 sequences (the sequences of one index of rep), no expert is named more than 4 times, and that count is reached; a token names different experts. `cache_len`: some sequence holds all 1024 cached tokens.
All inputs are finite; a program needn't handle non-finite values.
Results may differ from a plain program's by a relative error of at most 0.013.
Values may be sent and summed in bfloat16 or wider, within the bound.
A program may use at most 128 MiB of HBM per device.

v0:
```python
import math

import jax
import jax.numpy as jnp
from jax import lax
from jax.experimental import pallas as pl
from jax.experimental.pallas import tpu as pltpu
from jax.sharding import PartitionSpec as P

HD = 128


def attend_rows(queries, key_cache, value_cache, new_keys, new_values, cache_len):
    steps, rows, width = queries.shape
    cache = key_cache.shape[1]
    kv_heads = key_cache.shape[2] // HD
    group = width // HD // kv_heads
    scaling = 1.0 / math.sqrt(HD)
    heads = queries.reshape(steps, rows, kv_heads, group, HD).transpose(1, 2, 0, 3, 4)
    heads = heads.reshape(rows, kv_heads, steps * group, HD)
    keys = key_cache.reshape(rows, cache, kv_heads, HD)
    values = value_cache.reshape(rows, cache, kv_heads, HD)
    fresh_keys = new_keys.reshape(steps, rows, kv_heads, HD)
    fresh_values = new_values.reshape(steps, rows, kv_heads, HD)
    old = jnp.einsum("sjgd,stjd->sjgt", heads, keys, preferred_element_type=jnp.float32) * scaling
    new = (
        jnp.einsum("sjgd,tsjd->sjgt", heads, fresh_keys, preferred_element_type=jnp.float32)
        * scaling
    )
    position = lax.broadcasted_iota(jnp.int32, (1, 1, 1, cache), 3)
    old = jnp.where(position < cache_len[:, None, None, None], old, -1e30)
    step_of = lax.broadcasted_iota(jnp.int32, (1, 1, steps * group, steps), 2) // group
    fresh = lax.broadcasted_iota(jnp.int32, (1, 1, steps * group, steps), 3)
    new = jnp.where(fresh <= step_of, new, -1e30)
    top = jnp.maximum(
        jnp.max(old, axis=-1, keepdims=True), jnp.max(new, axis=-1, keepdims=True)
    )
    old, new = jnp.exp(old - top), jnp.exp(new - top)
    total = jnp.sum(old, axis=-1, keepdims=True) + jnp.sum(new, axis=-1, keepdims=True)
    old, new = (old / total).astype(jnp.bfloat16), (new / total).astype(jnp.bfloat16)
    out = jnp.einsum("sjgt,stjd->sjgd", old, values, preferred_element_type=jnp.float32)
    out = out + jnp.einsum(
        "sjgt,tsjd->sjgd", new, fresh_values, preferred_element_type=jnp.float32
    )
    out = out.reshape(rows, kv_heads, steps, group, HD).transpose(2, 0, 1, 3, 4)
    return out.reshape(steps, rows, width)


def norm_rows(hidden, norm_gain):
    mean_square = jnp.mean(hidden * hidden, axis=-1, keepdims=True)
    return (hidden * lax.rsqrt(mean_square + 1e-06) * norm_gain.astype(jnp.float32)).astype(
        jnp.bfloat16
    )


def per_device_plain(
    residual, queries, key_cache, value_cache, new_keys, new_values, cache_len, norm_gain,
    expert_ids, gate_scores, gate_weight, up_weight, down_weight,
):
    axes = ("rep", "exp")
    steps, rows, width = residual.shape
    local = gate_weight.shape[0]
    attention = attend_rows(queries, key_cache, value_cache, new_keys, new_values, cache_len)
    hidden = residual.astype(jnp.float32) + attention
    normed = norm_rows(hidden, norm_gain)
    scores = gate_scores.astype(jnp.float32)
    gates = scores / jnp.sum(scores, axis=-1, keepdims=True)
    tokens = lax.all_gather(normed.reshape(steps * rows, width), axes, axis=0, tiled=True)
    all_ids = lax.all_gather(expert_ids.reshape(steps * rows, -1), axes, axis=0, tiled=True)
    all_gates = lax.all_gather(gates.reshape(steps * rows, -1), axes, axis=0, tiled=True)
    mine = lax.axis_index("rep") * local + lax.broadcasted_iota(jnp.int32, (1, local, 1), 1)
    weight = jnp.sum(jnp.where(all_ids[:, None, :] == mine, all_gates[:, None, :], 0.0), axis=2)
    contract = (((1,), (1,)), ((), ()))
    units = gate_weight.shape[1]
    gate = lax.dot_general(
        tokens, gate_weight.reshape(local * units, width), contract,
        preferred_element_type=jnp.float32,
    )
    up = lax.dot_general(
        tokens, up_weight.reshape(local * units, width), contract,
        preferred_element_type=jnp.float32,
    )
    activation = (jax.nn.silu(gate) * up).reshape(-1, local, units) * weight[:, :, None]
    activation = activation.astype(jnp.bfloat16).reshape(-1, local * units)
    partial = jnp.dot(
        activation, down_weight.reshape(local * units, width), preferred_element_type=jnp.float32
    ).astype(jnp.bfloat16)
    mixed = lax.psum_scatter(partial, axes, scatter_dimension=0, tiled=True)
    mixed = mixed.reshape(steps, rows, width).astype(jnp.float32)
    return (hidden + mixed).astype(jnp.bfloat16)


CHUNKS = 4
ROWS = 8
DEVICES = 32
MESH = pl.DeviceIdType.MESH
F32 = jnp.float32
BF16 = jnp.bfloat16
NT = (((1,), (1,)), ((), ()))


def attend_in_vmem(
    q_ref, k_ref, v_ref, nk_ref, nv_ref, len_ref, heads, fresh_k, fresh_v, att
):
    steps, seqs, width = q_ref.shape
    cache = k_ref.shape[1]
    kv_heads = k_ref.shape[2] // HD
    head_count = width // HD
    group = head_count // kv_heads
    scaling = 1.0 / math.sqrt(HD)
    for step in range(steps):
        rows = q_ref[step].astype(F32)
        for h in range(head_count):
            heads[step * seqs : (step + 1) * seqs, h, :] = rows[:, h * HD : (h + 1) * HD]
    fresh_k[...] = jnp.zeros_like(fresh_k)
    fresh_v[...] = jnp.zeros_like(fresh_v)
    for step in range(steps):
        key_rows = nk_ref[step].astype(F32)
        value_rows = nv_ref[step].astype(F32)
        for seq in range(seqs):
            for j in range(kv_heads):
                cols = slice(j * HD, (j + 1) * HD)
                at = seq * kv_heads + j
                fresh_k[at, step : step + 1, :] = key_rows[seq : seq + 1, cols]
                fresh_v[at, step : step + 1, :] = value_rows[seq : seq + 1, cols]
    total = steps * group
    position = lax.broadcasted_iota(jnp.int32, (total, cache), 1)
    fresh_at = lax.broadcasted_iota(jnp.int32, (total, HD), 1)
    step_of = lax.broadcasted_iota(jnp.int32, (total, HD), 0) // group
    for seq in range(seqs):
        valid = position < len_ref[seq]
        for j in range(kv_heads):
            at = seq * kv_heads + j
            cols = slice(j * HD, (j + 1) * HD)
            query = jnp.concatenate(
                [
                    heads[step * seqs + seq, j * group : (j + 1) * group, :]
                    for step in range(steps)
                ],
                axis=0,
            ).astype(BF16)
            old = lax.dot_general(query, k_ref[seq, :, cols], NT, preferred_element_type=F32)
            new = lax.dot_general(
                query, fresh_k[at].astype(BF16), NT, preferred_element_type=F32
            )
            old = jnp.where(valid, old * scaling, -1e30)
            new = jnp.where(fresh_at <= step_of, new * scaling, -1e30)
            top = jnp.maximum(
                jnp.max(old, axis=-1, keepdims=True), jnp.max(new, axis=-1, keepdims=True)
            )
            old, new = jnp.exp(old - top), jnp.exp(new - top)
            share = 1.0 / (
                jnp.sum(old, axis=-1, keepdims=True) + jnp.sum(new, axis=-1, keepdims=True)
            )
            old, new = (old * share).astype(BF16), (new * share).astype(BF16)
            out = jnp.dot(old, v_ref[seq, :, cols], preferred_element_type=F32)
            out = out + jnp.dot(new, fresh_v[at].astype(BF16), preferred_element_type=F32)
            for step in range(steps):
                att[step * seqs + seq, j * group : (j + 1) * group, :] = out[
                    step * group : (step + 1) * group
                ]


def layer_kernel(
    res_ref, q_ref, k_ref, v_ref, nk_ref, nv_ref, len_ref, gain_ref, ids_ref, score_ref,
    gate_hbm, up_hbm, down_hbm,
    out_ref,
    wg, wu, wd, heads, fresh_k, fresh_v, att, hid, own_gates, x, gates, xk, g_acc, u_acc, act,
    p, rc, r1, r2, rz, w_sem, ag_send, ag_recv, rs_send, rs_recv,
):
    steps, seqs, width = res_ref.shape
    local, units = gate_hbm.shape[0], gate_hbm.shape[1]
    cols = width // CHUNKS
    rep, y = lax.axis_index("rep"), lax.axis_index("exp")
    c = lax.rem(rep, 2)
    xx = lax.rem(lax.div(rep, 2), 2)
    z = lax.div(rep, 4)

    def device(z_at, x_at, c_at, y_at):
        return ((z_at * 2 + x_at) * 2 + c_at, y_at)

    def group(c_at, x_at, y_at):
        return ((c_at * 2 + x_at) * 2 + y_at) * 4

    px, py, pc = device(z, 1 - xx, c, y), device(z, xx, c, 1 - y), device(z, xx, 1 - c, y)
    zs = [lax.rem(z + dz, 4) for dz in range(4)]
    pz = [device(at, xx, c, y) for at in zs]
    mine = group(c, xx, y)
    me = mine + z

    weights = []
    for k in range(CHUNKS):
        at = pl.ds(k * cols, cols)
        weights.append(
            [
                pltpu.make_async_copy(gate_hbm.at[:, :, at], wg.at[k], w_sem.at[0, k]),
                pltpu.make_async_copy(up_hbm.at[:, :, at], wu.at[k], w_sem.at[1, k]),
            ]
        )
    downs = [
        pltpu.make_async_copy(
            down_hbm.at[:, :, pl.ds(k * cols, cols)], wd.at[k], w_sem.at[2, k]
        )
        for k in range(CHUNKS)
    ]
    for pair in weights:
        for copy in pair:
            copy.start()
    for copy in downs:
        copy.start()

    barrier = pltpu.get_barrier_semaphore()
    for peer in (px, py, pc, pz[1], pz[2], pz[3]):
        pl.semaphore_signal(barrier, inc=1, device_id=peer, device_id_type=MESH)

    attend_in_vmem(
        q_ref, k_ref, v_ref, nk_ref, nv_ref, len_ref, heads, fresh_k, fresh_v, att
    )
    hid[...] = jnp.zeros_like(hid)
    for h in range(width // HD):
        hid[0 : steps * seqs, h * HD : (h + 1) * HD] = att[:, h, :]
    for step in range(steps):
        at = slice(step * seqs, (step + 1) * seqs)
        hid[at, :] = hid[at, :] + res_ref[step].astype(F32)
    hidden = hid[...]
    mean_square = jnp.mean(hidden * hidden, axis=-1, keepdims=True)
    normed = (hidden * lax.rsqrt(mean_square + 1e-06) * gain_ref[...].astype(F32)).astype(BF16)
    for k in range(CHUNKS):
        x[k, me] = normed[:, k * cols : (k + 1) * cols]
    own_gates[...] = jnp.zeros_like(own_gates)
    lane = lax.broadcasted_iota(jnp.int32, (seqs, HD), 1)
    for step in range(steps):
        chosen = ids_ref[step]
        score = score_ref[step].astype(F32)
        score = score / jnp.sum(score, axis=-1, keepdims=True)
        spread = jnp.zeros((seqs, HD), F32)
        for place in range(chosen.shape[1]):
            spread = spread + jnp.where(
                lane == chosen[:, place : place + 1], score[:, place : place + 1], 0.0
            )
        own_gates[step * seqs : (step + 1) * seqs, :] = spread
    gates[me] = own_gates[...]

    started = []

    def send(src, dst, sems, i, j, peer):
        copy = pltpu.make_async_remote_copy(
            src_ref=src, dst_ref=dst, send_sem=sems[0].at[i, j], recv_sem=sems[1].at[i, j],
            device_id=peer, device_id_type=MESH,
        )
        copy.start()
        started.append(copy)

    def arrive(ref, sems, i, j, peer):
        pltpu.make_async_remote_copy(
            src_ref=ref, dst_ref=ref, send_sem=sems[0].at[i, j], recv_sem=sems[1].at[i, j],
            device_id=peer, device_id_type=MESH,
        ).wait_recv()

    ag, rs = (ag_send, ag_recv), (rs_send, rs_recv)
    pl.semaphore_wait(barrier, 6)

    parts = [x.at[0], gates] + [x.at[k] for k in range(1, CHUNKS)]
    own, side_x = pl.ds(mine, 4), pl.ds(group(c, 1 - xx, y), 4)
    side_y, corner = pl.ds(group(c, xx, 1 - y), 4), pl.ds(group(c, 1 - xx, 1 - y), 4)
    others = [
        pl.ds(group(1 - c, xx, y), 4), pl.ds(group(1 - c, 1 - xx, y), 4),
        pl.ds(group(1 - c, xx, 1 - y), 4), pl.ds(group(1 - c, 1 - xx, 1 - y), 4),
    ]

    def gather_z(i):
        for dz in (1, 2, 3):
            send(parts[i].at[me], parts[i].at[me], ag, i, dz, pz[dz])

    def gather_a(i):
        for dz in (1, 2, 3):
            back = lax.rem(z + 4 - dz, 4)
            arrive(parts[i].at[mine + back], ag, i, dz, pz[4 - dz])
        send(parts[i].at[own], parts[i].at[own], ag, i, 4, px)
        send(parts[i].at[own], parts[i].at[own], ag, i, 5, py)
        send(parts[i].at[own], parts[i].at[own], ag, i, 6, pc)

    def gather_b(i):
        arrive(parts[i].at[side_x], ag, i, 4, px)
        if i % 2 == 0:
            send(parts[i].at[side_x], parts[i].at[side_x], ag, i, 0, py)
        send(parts[i].at[side_x], parts[i].at[side_x], ag, i, 7, pc)
        arrive(parts[i].at[side_y], ag, i, 5, py)
        if i % 2 == 1:
            send(parts[i].at[side_y], parts[i].at[side_y], ag, i, 0, px)
        send(parts[i].at[side_y], parts[i].at[side_y], ag, i, 8, pc)

    def gather_c(i):
        arrive(parts[i].at[corner], ag, i, 0, py if i % 2 == 0 else px)
        send(parts[i].at[corner], parts[i].at[corner], ag, i, 9, pc)

    def gather_d(i):
        for n, at in enumerate(others):
            arrive(parts[i].at[at], ag, i, 6 + n, pc)

    def project(k):
        for copy in weights[k]:
            copy.wait()
        xk[...] = x[k].astype(F32).reshape(DEVICES * ROWS, cols).astype(BF16)

        @pl.loop(0, local)
        def _(e):
            tokens = xk[...]
            g = lax.dot_general(wg[k, e], tokens, NT, preferred_element_type=F32)
            u = lax.dot_general(wu[k, e], tokens, NT, preferred_element_type=F32)
            if k == 0:
                g_acc[e] = g
                u_acc[e] = u
            else:
                g_acc[e] += g
                u_acc[e] += u

    count = len(parts)
    for i in range(count):
        gather_z(i)
    for t in range(count + 3):
        if t < count:
            gather_a(t)
        if 0 <= t - 1 < count:
            gather_b(t - 1)
        if 0 <= t - 2 < count:
            gather_c(t - 2)
        if 0 <= t - 3 < count:
            i = t - 3
            gather_d(i)
            if i != 1:
                project(0 if i == 0 else i - 1)

    by_expert = gates[...].reshape(DEVICES * ROWS, HD).T
    row = lax.broadcasted_iota(jnp.int32, by_expert.shape, 0)
    tile = 256
    for e in range(local):
        gate_row = jnp.sum(
            jnp.where(row == rep * local + e, by_expert, 0.0), axis=0, keepdims=True
        )
        for n in range(units // tile):
            at = slice(n * tile, (n + 1) * tile)
            g, u = g_acc[e, at, :], u_acc[e, at, :]
            value = g / (1.0 + jnp.exp(-g)) * u * gate_row
            act[:, e * units + n * tile : e * units + (n + 1) * tile] = value.T.astype(BF16)

    half = cols // 2

    def reduce_0(n):
        downs[n].wait()

        for h in range(2):
            at = slice(h * half, (h + 1) * half)
            part = jnp.dot(act[:, 0:units], wd[n, 0, :, at], preferred_element_type=F32)
            for e in range(1, local):
                part = part + jnp.dot(
                    act[:, e * units : (e + 1) * units], wd[n, e, :, at],
                    preferred_element_type=F32,
                )
            p[n, :, :, at] = part.reshape(DEVICES, ROWS, half).astype(BF16)
        send(p.at[n, pl.ds((1 - c) * 16, 16)], rc.at[n], rs, n, 0, pc)

    def add(target, values):
        total = target[...].astype(F32)
        for value in values:
            total = total + value[...].astype(F32)
        target[...] = total.astype(BF16)

    def reduce_1(n):
        arrive(rc.at[n], rs, n, 0, pc)
        add(p.at[n, pl.ds(c * 16, 16)], [rc.at[n]])
        peer, near = (px, side_x) if n % 2 == 0 else (py, side_y)
        send(p.at[n, corner], r1.at[n, 0], rs, n, 1, peer)
        send(p.at[n, near], r1.at[n, 1], rs, n, 2, peer)

    def reduce_2(n):
        peer = px if n % 2 == 0 else py
        arrive(r1.at[n, 0], rs, n, 1, peer)
        onward, far = (py, side_y) if n % 2 == 0 else (px, side_x)
        add(p.at[n, far], [r1.at[n, 0]])
        send(p.at[n, far], r2.at[n], rs, n, 3, onward)

    def reduce_3(n):
        arrive(r1.at[n, 1], rs, n, 2, px if n % 2 == 0 else py)
        arrive(r2.at[n], rs, n, 3, py if n % 2 == 0 else px)
        add(p.at[n, own], [r1.at[n, 1], r2.at[n]])
        for dz in (1, 2, 3):
            send(p.at[n, mine + zs[dz]], rz.at[n, dz], rs, n, 3 + dz, pz[dz])

    def reduce_4(n):
        at = slice(n * cols, (n + 1) * cols)
        total = p[n, me].astype(F32)
        for dz in (1, 2, 3):
            arrive(rz.at[n, dz], rs, n, 3 + dz, pz[4 - dz])
            total = total + rz[n, dz].astype(F32)
        total = total + hid[:, at]
        for step in range(steps):
            out_ref[step, :, at] = total[step * seqs : (step + 1) * seqs].astype(BF16)

    stages = (reduce_0, reduce_1, reduce_2, reduce_3, reduce_4)
    for t in range(CHUNKS + len(stages) - 1):
        for lag, stage in enumerate(stages):
            if 0 <= t - lag < CHUNKS:
                stage(t - lag)
    for copy in started:
        copy.wait_send()


def per_device_kernel(
    residual, queries, key_cache, value_cache, new_keys, new_values, cache_len, norm_gain,
    expert_ids, gate_scores, gate_weight, up_weight, down_weight,
):
    steps, seqs, width = residual.shape
    local, units, _ = gate_weight.shape
    cols = width // CHUNKS
    kv_heads = key_cache.shape[2] // HD
    heads = width // HD
    vmem = pl.BlockSpec(memory_space=pltpu.VMEM)
    hbm = pl.BlockSpec(memory_space=pl.ANY)
    smem = pl.BlockSpec(memory_space=pltpu.SMEM)
    rows = DEVICES * ROWS
    return pl.pallas_call(
        layer_kernel,
        out_shape=jax.ShapeDtypeStruct(residual.shape, BF16),
        in_specs=[vmem] * 6 + [smem] + [vmem] * 3 + [hbm] * 3,
        out_specs=vmem,
        scratch_shapes=[
            pltpu.VMEM((CHUNKS, local, units, cols), BF16),
            pltpu.VMEM((CHUNKS, local, units, cols), BF16),
            pltpu.VMEM((CHUNKS, local, units, cols), BF16),
            pltpu.VMEM((steps * seqs, heads, HD), F32),
            pltpu.VMEM((seqs * kv_heads, HD, HD), F32),
            pltpu.VMEM((seqs * kv_heads, HD, HD), F32),
            pltpu.VMEM((steps * seqs, heads, HD), F32),
            pltpu.VMEM((ROWS, width), F32),
            pltpu.VMEM((ROWS, HD), F32),
            pltpu.VMEM((CHUNKS, DEVICES, ROWS, cols), BF16),
            pltpu.VMEM((DEVICES, ROWS, HD), F32),
            pltpu.VMEM((rows, cols), BF16),
            pltpu.VMEM((local, units, rows), F32),
            pltpu.VMEM((local, units, rows), F32),
            pltpu.VMEM((rows, local * units), BF16),
            pltpu.VMEM((CHUNKS, DEVICES, ROWS, cols), BF16),
            pltpu.VMEM((CHUNKS, 16, ROWS, cols), BF16),
            pltpu.VMEM((CHUNKS, 2, 4, ROWS, cols), BF16),
            pltpu.VMEM((CHUNKS, 4, ROWS, cols), BF16),
            pltpu.VMEM((CHUNKS, 4, ROWS, cols), BF16),
            pltpu.SemaphoreType.DMA((3, CHUNKS)),
            pltpu.SemaphoreType.DMA((CHUNKS + 1, 10)),
            pltpu.SemaphoreType.DMA((CHUNKS + 1, 10)),
            pltpu.SemaphoreType.DMA((CHUNKS, 7)),
            pltpu.SemaphoreType.DMA((CHUNKS, 7)),
        ],
        compiler_params=pltpu.CompilerParams(
            collective_id=0, has_side_effects=True, vmem_limit_bytes=60 * 1024 * 1024
        ),
    )(
        residual, queries, key_cache, value_cache, new_keys, new_values, cache_len,
        norm_gain.reshape(1, width), expert_ids, gate_scores, gate_weight, up_weight,
        down_weight,
    )


def solution(mesh):
    in_specs = (
        P(None, ("rep", "exp"), None),
        P(None, ("rep", "exp"), None),
        P(("rep", "exp"), None, None),
        P(("rep", "exp"), None, None),
        P(None, ("rep", "exp"), None),
        P(None, ("rep", "exp"), None),
        P(("rep", "exp")),
        P(),
        P(None, ("rep", "exp"), None),
        P(None, ("rep", "exp"), None),
        P("rep", "exp", None),
        P("rep", "exp", None),
        P("rep", "exp", None),
    )
    out_specs = P(None, ("rep", "exp"), None)
    fits = mesh.shape["rep"] == 16 and mesh.shape["exp"] == 2
    per_device = per_device_kernel if fits else per_device_plain
    return jax.shard_map(
        per_device, mesh=mesh, in_specs=in_specs, out_specs=out_specs, check_vma=False
    )
```

profile of v0, /device:TPU:0, one launch (start us, length us, event | category | flops | bytes accessed | tf_op | source)
XLA Modules:
  0.0 60.6 jit_solution(1501078918894505475)
XLA Ops:
  0.0 1.3 %reshape.3.gain_ref = bf16[1,4096]{1,0:T(2,128)(2,1)} reshape(bf16[4096]{0:T(1024)(128)(2,1)} %param.20) | data formatting | bytes 16384 | tf_op jit(solution)/shard_map/reshape | solution.py:459
  1.3 57.8 %shard_map.127 = bf16[3,2,4096]{2,1,0:T(2,128)(2,1)} custom-call(bf16[3,2,4096]{2,1,0:T(2,128)(2,1)} %res_ref.1, bf16[3,2,4096]{2,1,0:T(2,128)(2,1)} %q_ref.1, bf16[2,1024,256]{2,1,0:T(8,128)(2,1)} %k_ref.1, bf16[2,1024,256]{2,1,0:T(8,128)(2,1)} %v_ref.1, bf16[3,2,256]{2,1,0:T(2,128)(2,1)} %nk_ref.1, bf16[3,2,256]{2,1,0:T(2,128)(2,1)} %nv_ref.1, s32[2]{0:T(128)} %len_ref.1, ...), custom_call_target="tpu_custom_call" | custom-call | tf_op jit(solution)/shard_map/pallas_call | solution.py:422
  59.1 1.5 %copy.15 = bf16[3,2,4096]{2,1,0:T(2,128)(2,1)} copy(bf16[3,2,4096]{2,1,0:T(2,128)(2,1)} %shard_map.127) | data formatting | bytes 98304
where the time goes:
time: 60.8 us; the launch traced here: 60.6 us
  Pallas kernels  57.8 us (95%)
  local copies, waits for them, and re-layouts  2.76 us (5%)
    pallas_call x1, Pallas kernels, per_device_kernel(): pl.pallas_call(layer_kernel, out_shape=jax.ShapeDtypeStruct(residual.shap...  57.8 us
    unnamed x1, local copies, waits for them, and re-layouts  1.45 us
    reshape x1, local copies, waits for them, and re-layouts, per_device_kernel(): norm_gain.reshape(1, width)  1.31 us

commit v1 on v0

--- a/solution.py
+++ b/solution.py
@@ -224,7 +224,9 @@
         hid[at, :] = hid[at, :] + res_ref[step].astype(F32)
     hidden = hid[...]
     mean_square = jnp.mean(hidden * hidden, axis=-1, keepdims=True)
-    normed = (hidden * lax.rsqrt(mean_square + 1e-06) * gain_ref[...].astype(F32)).astype(BF16)
+    normed = (hidden * lax.rsqrt(mean_square + 1e-06) * gain_ref[...].astype(F32).reshape(1, width)).astype(
+        BF16
+    )
     for k in range(CHUNKS):
         x[k, me] = normed[:, k * cols : (k + 1) * cols]
     own_gates[...] = jnp.zeros_like(own_gates)
@@ -260,7 +262,7 @@
     ag, rs = (ag_send, ag_recv), (rs_send, rs_recv)
     pl.semaphore_wait(barrier, 6)
 
-    parts = [x.at[0], gates] + [x.at[k] for k in range(1, CHUNKS)]
+    parts = [x.at[k] for k in range(CHUNKS)] + [gates]
     own, side_x = pl.ds(mine, 4), pl.ds(group(c, 1 - xx, y), 4)
     side_y, corner = pl.ds(group(c, xx, 1 - y), 4), pl.ds(group(c, 1 - xx, 1 - y), 4)
     others = [
@@ -315,34 +317,41 @@
                 g_acc[e] += g
                 u_acc[e] += u
 
-    count = len(parts)
-    for i in range(count):
+    def project_last(k):
+        for copy in weights[k]:
+            copy.wait()
+        xk[...] = x[k].astype(F32).reshape(DEVICES * ROWS, cols).astype(BF16)
+        by_expert = gates[...].reshape(DEVICES * ROWS, HD).T
+        row = lax.broadcasted_iota(jnp.int32, by_expert.shape, 0)
+        tokens = xk[...]
+        tile = 256
+        for e in range(local):
+            gate_row = jnp.sum(
+                jnp.where(row == rep * local + e, by_expert, 0.0), axis=0, keepdims=True
+            )
+            g_all = lax.dot_general(wg[k, e], tokens, NT, preferred_element_type=F32)
+            u_all = lax.dot_general(wu[k, e], tokens, NT, preferred_element_type=F32)
+            for n in range(units // tile):
+                at = slice(n * tile, (n + 1) * tile)
+                g, u = g_acc[e, at, :] + g_all[at], u_acc[e, at, :] + u_all[at]
+                value = g / (1.0 + jnp.exp(-g)) * u * gate_row
+                first = e * units + n * tile
+                act[:, first : first + tile] = value.T.astype(BF16)
+
+    turns = [[0, CHUNKS]] + [[k] for k in range(1, CHUNKS)]
+    for i in turns[0]:
         gather_z(i)
-    for t in range(count + 3):
-        if t < count:
-            gather_a(t)
-        if 0 <= t - 1 < count:
-            gather_b(t - 1)
-        if 0 <= t - 2 < count:
-            gather_c(t - 2)
-        if 0 <= t - 3 < count:
-            i = t - 3
-            gather_d(i)
-            if i != 1:
-                project(0 if i == 0 else i - 1)
-
-    by_expert = gates[...].reshape(DEVICES * ROWS, HD).T
-    row = lax.broadcasted_iota(jnp.int32, by_expert.shape, 0)
-    tile = 256
-    for e in range(local):
-        gate_row = jnp.sum(
-            jnp.where(row == rep * local + e, by_expert, 0.0), axis=0, keepdims=True
-        )
-        for n in range(units // tile):
-            at = slice(n * tile, (n + 1) * tile)
-            g, u = g_acc[e, at, :], u_acc[e, at, :]
-            value = g / (1.0 + jnp.exp(-g)) * u * gate_row
-            act[:, e * units + n * tile : e * units + (n + 1) * tile] = value.T.astype(BF16)
+    for t in range(CHUNKS + 3):
+        if t + 1 < CHUNKS:
+            for i in turns[t + 1]:
+                gather_z(i)
+        for lag, stage in enumerate((gather_a, gather_b, gather_c, gather_d)):
+            if 0 <= t - lag < CHUNKS:
+                for i in turns[t - lag]:
+                    stage(i)
+        if 0 <= t - 3 < CHUNKS - 1:
+            project(t - 3)
+    project_last(CHUNKS - 1)
 
     half = cols // 2
 
@@ -456,7 +465,7 @@
         ),
     )(
         residual, queries, key_cache, value_cache, new_keys, new_values, cache_len,
-        norm_gain.reshape(1, width), expert_ids, gate_scores, gate_weight, up_weight,
+        norm_gain, expert_ids, gate_scores, gate_weight, up_weight,
         down_weight,
     )
 

time: 60.8 us -> 55.1 us (0.906)
  Pallas kernels: 57.8 us -> 53.5 us
  local copies, waits for them, and re-layouts: 2.76 us -> 1.45 us
    pallas_call x1, Pallas kernels: 57.8 us -> 53.5 us  [per_device_kernel(): pl.pallas_call(layer_kernel, out_shape=jax.ShapeDtypeStruct(residual.shap...]
    reshape x1 -> x0, local copies, waits for them, and re-layouts: 1.31 us -> none  [per_device_kernel(): norm_gain.reshape(1, width)]
where the time goes in v1:
time: 55.1 us; the launch traced here: 54.9 us
  Pallas kernels  53.5 us (97%)
  local copies, waits for them, and re-layouts  1.45 us (3%)
    pallas_call x1, Pallas kernels, per_device_kernel(): pl.pallas_call(layer_kernel, out_shape=jax.ShapeDtypeStruct(residual.shap...  53.5 us
    unnamed x1, local copies, waits for them, and re-layouts  1.45 us

profile of v1, /device:TPU:0, one launch (start us, length us, event | category | flops | bytes accessed | tf_op | source)
XLA Modules:
  0.0 54.9 jit_solution(8260691152376347426)
XLA Ops:
  0.0 53.5 %shard_map.127 = bf16[3,2,4096]{2,1,0:T(2,128)(2,1)} custom-call(bf16[3,2,4096]{2,1,0:T(2,128)(2,1)} %res_ref.1, bf16[3,2,4096]{2,1,0:T(2,128)(2,1)} %q_ref.1, bf16[2,1024,256]{2,1,0:T(8,128)(2,1)} %k_ref.1, bf16[2,1024,256]{2,1,0:T(8,128)(2,1)} %v_ref.1, bf16[3,2,256]{2,1,0:T(2,128)(2,1)} %nk_ref.1, bf16[3,2,256]{2,1,0:T(2,128)(2,1)} %nv_ref.1, s32[2]{0:T(128)} %len_ref.1, ...), custom_call_target="tpu_custom_call" | custom-call | tf_op jit(solution)/shard_map/pallas_call | solution.py:431
  53.5 1.5 %copy.15 = bf16[3,2,4096]{2,1,0:T(2,128)(2,1)} copy(bf16[3,2,4096]{2,1,0:T(2,128)(2,1)} %shard_map.127) | data formatting | bytes 98304

commit v2 on v1

--- a/solution.py
+++ b/solution.py
@@ -282,18 +282,27 @@
         send(parts[i].at[own], parts[i].at[own], ag, i, 5, py)
         send(parts[i].at[own], parts[i].at[own], ag, i, 6, pc)
 
+    half = cols // 2
+    halves = [pl.ds(h * half, half) for h in range(2)]
+
+    def routed(i, rows):
+        if i == CHUNKS:
+            return [parts[i].at[rows]]
+        return [parts[i].at[rows, :, at] for at in halves]
+
     def gather_b(i):
         arrive(parts[i].at[side_x], ag, i, 4, px)
-        if i % 2 == 0:
-            send(parts[i].at[side_x], parts[i].at[side_x], ag, i, 0, py)
+        block = routed(i, side_x)[0]
+        send(block, block, ag, i, 0, py)
         send(parts[i].at[side_x], parts[i].at[side_x], ag, i, 7, pc)
         arrive(parts[i].at[side_y], ag, i, 5, py)
-        if i % 2 == 1:
-            send(parts[i].at[side_y], parts[i].at[side_y], ag, i, 0, px)
+        for block in routed(i, side_y)[1:]:
+            send(block, block, ag, i, 10, px)
         send(parts[i].at[side_y], parts[i].at[side_y], ag, i, 8, pc)
 
     def gather_c(i):
-        arrive(parts[i].at[corner], ag, i, 0, py if i % 2 == 0 else px)
+        for block, at, peer in zip(routed(i, corner), (0, 10), (py, px)):
+            arrive(block, ag, i, at, peer)
         send(parts[i].at[corner], parts[i].at[corner], ag, i, 9, pc)
 
     def gather_d(i):
@@ -353,8 +362,6 @@
             project(t - 3)
     project_last(CHUNKS - 1)
 
-    half = cols // 2
-
     def reduce_0(n):
         downs[n].wait()
 
@@ -378,29 +385,34 @@
     def reduce_1(n):
         arrive(rc.at[n], rs, n, 0, pc)
         add(p.at[n, pl.ds(c * 16, 16)], [rc.at[n]])
-        peer, near = (px, side_x) if n % 2 == 0 else (py, side_y)
-        send(p.at[n, corner], r1.at[n, 0], rs, n, 1, peer)
-        send(p.at[n, near], r1.at[n, 1], rs, n, 2, peer)
+        for h, (peer, near) in enumerate(((px, side_x), (py, side_y))):
+            at = halves[h]
+            send(p.at[n, corner, :, at], r1.at[n, 0, :, :, at], rs, n, 1 + h, peer)
+        for h, (peer, near) in enumerate(((px, side_x), (py, side_y))):
+            at = halves[h]
+            send(p.at[n, near, :, at], r1.at[n, 1, :, :, at], rs, n, 3 + h, peer)
 
     def reduce_2(n):
-        peer = px if n % 2 == 0 else py
-        arrive(r1.at[n, 0], rs, n, 1, peer)
-        onward, far = (py, side_y) if n % 2 == 0 else (px, side_x)
-        add(p.at[n, far], [r1.at[n, 0]])
-        send(p.at[n, far], r2.at[n], rs, n, 3, onward)
+        for h, (peer, onward, far) in enumerate(((px, py, side_y), (py, px, side_x))):
+            at = halves[h]
+            arrive(r1.at[n, 0, :, :, at], rs, n, 1 + h, peer)
+            add(p.at[n, far, :, at], [r1.at[n, 0, :, :, at]])
+            send(p.at[n, far, :, at], r2.at[n, :, :, at], rs, n, 5 + h, onward)
 
     def reduce_3(n):
-        arrive(r1.at[n, 1], rs, n, 2, px if n % 2 == 0 else py)
-        arrive(r2.at[n], rs, n, 3, py if n % 2 == 0 else px)
+        for h, (peer, onward) in enumerate(((px, py), (py, px))):
+            at = halves[h]
+            arrive(r1.at[n, 1, :, :, at], rs, n, 3 + h, peer)
+            arrive(r2.at[n, :, :, at], rs, n, 5 + h, onward)
         add(p.at[n, own], [r1.at[n, 1], r2.at[n]])
         for dz in (1, 2, 3):
-            send(p.at[n, mine + zs[dz]], rz.at[n, dz], rs, n, 3 + dz, pz[dz])
+            send(p.at[n, mine + zs[dz]], rz.at[n, dz], rs, n, 6 + dz, pz[dz])
 
     def reduce_4(n):
         at = slice(n * cols, (n + 1) * cols)
         total = p[n, me].astype(F32)
         for dz in (1, 2, 3):
-            arrive(rz.at[n, dz], rs, n, 3 + dz, pz[4 - dz])
+            arrive(rz.at[n, dz], rs, n, 6 + dz, pz[4 - dz])
             total = total + rz[n, dz].astype(F32)
         total = total + hid[:, at]
         for step in range(steps):
@@ -455,10 +467,10 @@
             pltpu.VMEM((CHUNKS, 4, ROWS, cols), BF16),
             pltpu.VMEM((CHUNKS, 4, ROWS, cols), BF16),
             pltpu.SemaphoreType.DMA((3, CHUNKS)),
-            pltpu.SemaphoreType.DMA((CHUNKS + 1, 10)),
-            pltpu.SemaphoreType.DMA((CHUNKS + 1, 10)),
-            pltpu.SemaphoreType.DMA((CHUNKS, 7)),
-            pltpu.SemaphoreType.DMA((CHUNKS, 7)),
+            pltpu.SemaphoreType.DMA((CHUNKS + 1, 11)),
+            pltpu.SemaphoreType.DMA((CHUNKS + 1, 11)),
+            pltpu.SemaphoreType.DMA((CHUNKS, 10)),
+            pltpu.SemaphoreType.DMA((CHUNKS, 10)),
         ],
         compiler_params=pltpu.CompilerParams(
             collective_id=0, has_side_effects=True, vmem_limit_bytes=60 * 1024 * 1024

time: 55.1 us -> 53 us (0.962)
  Pallas kernels: 53.5 us -> 51.4 us
    pallas_call x1, Pallas kernels: 53.5 us -> 51.4 us  [per_device_kernel(): pl.pallas_call(layer_kernel, out_shape=jax.ShapeDtypeStruct(residual.shap...]
where the time goes in v2:
time: 53 us; the launch traced here: 52.8 us
  Pallas kernels  51.4 us (97%)
  local copies, waits for them, and re-layouts  1.45 us (3%)
    pallas_call x1, Pallas kernels, per_device_kernel(): pl.pallas_call(layer_kernel, out_shape=jax.ShapeDtypeStruct(residual.shap...  51.4 us
    unnamed x1, local copies, waits for them, and re-layouts  1.45 us

profile of v2, /device:TPU:0, one launch (start us, length us, event | category | flops | bytes accessed | tf_op | source)
XLA Modules:
  0.0 52.8 jit_solution(2425763694165268109)
XLA Ops:
  0.0 51.4 %shard_map.127 = bf16[3,2,4096]{2,1,0:T(2,128)(2,1)} custom-call(bf16[3,2,4096]{2,1,0:T(2,128)(2,1)} %res_ref.1, bf16[3,2,4096]{2,1,0:T(2,128)(2,1)} %q_ref.1, bf16[2,1024,256]{2,1,0:T(8,128)(2,1)} %k_ref.1, bf16[2,1024,256]{2,1,0:T(8,128)(2,1)} %v_ref.1, bf16[3,2,256]{2,1,0:T(2,128)(2,1)} %nk_ref.1, bf16[3,2,256]{2,1,0:T(2,128)(2,1)} %nv_ref.1, s32[2]{0:T(128)} %len_ref.1, ...), custom_call_target="tpu_custom_call" | custom-call | tf_op jit(solution)/shard_map/pallas_call | solution.py:443
  51.4 1.5 %copy.15 = bf16[3,2,4096]{2,1,0:T(2,128)(2,1)} copy(bf16[3,2,4096]{2,1,0:T(2,128)(2,1)} %shard_map.127) | data formatting | bytes 98304

commit v3 on v2

--- a/solution.py
+++ b/solution.py
@@ -100,7 +100,7 @@
 
 
 def attend_in_vmem(
-    q_ref, k_ref, v_ref, nk_ref, nv_ref, len_ref, heads, fresh_k, fresh_v, att
+    q_ref, k_ref, v_ref, nk_ref, nv_ref, len_ref, heads, fresh_k, fresh_v, att, caches
 ):
     steps, seqs, width = q_ref.shape
     cache = k_ref.shape[1]
@@ -123,6 +123,8 @@
                 at = seq * kv_heads + j
                 fresh_k[at, step : step + 1, :] = key_rows[seq : seq + 1, cols]
                 fresh_v[at, step : step + 1, :] = value_rows[seq : seq + 1, cols]
+    for copy in caches:
+        copy.wait()
     total = steps * group
     position = lax.broadcasted_iota(jnp.int32, (total, cache), 1)
     fresh_at = lax.broadcasted_iota(jnp.int32, (total, HD), 1)
@@ -162,10 +164,10 @@
 
 
 def layer_kernel(
-    res_ref, q_ref, k_ref, v_ref, nk_ref, nv_ref, len_ref, gain_ref, ids_ref, score_ref,
+    res_ref, q_ref, k_hbm, v_hbm, nk_ref, nv_ref, len_ref, gain_ref, ids_ref, score_ref,
     gate_hbm, up_hbm, down_hbm,
     out_ref,
-    wg, wu, wd, heads, fresh_k, fresh_v, att, hid, own_gates, x, gates, xk, g_acc, u_acc, act,
+    k_ref, v_ref, wg, wu, wd, heads, fresh_k, fresh_v, att, hid, own_gates, x, gates, xk, g_acc, u_acc, act,
     p, rc, r1, r2, rz, w_sem, ag_send, ag_recv, rs_send, rs_recv,
 ):
     steps, seqs, width = res_ref.shape
@@ -188,6 +190,12 @@
     mine = group(c, xx, y)
     me = mine + z
 
+    caches = [
+        pltpu.make_async_copy(k_hbm, k_ref, w_sem.at[3, 0]),
+        pltpu.make_async_copy(v_hbm, v_ref, w_sem.at[3, 1]),
+    ]
+    for copy in caches:
+        copy.start()
     weights = []
     for k in range(CHUNKS):
         at = pl.ds(k * cols, cols)
@@ -214,7 +222,7 @@
         pl.semaphore_signal(barrier, inc=1, device_id=peer, device_id_type=MESH)
 
     attend_in_vmem(
-        q_ref, k_ref, v_ref, nk_ref, nv_ref, len_ref, heads, fresh_k, fresh_v, att
+        q_ref, k_ref, v_ref, nk_ref, nv_ref, len_ref, heads, fresh_k, fresh_v, att, caches
     )
     hid[...] = jnp.zeros_like(hid)
     for h in range(width // HD):
@@ -416,7 +424,7 @@
             total = total + rz[n, dz].astype(F32)
         total = total + hid[:, at]
         for step in range(steps):
-            out_ref[step, :, at] = total[step * seqs : (step + 1) * seqs].astype(BF16)
+            out_ref[step, :, at] = total[step * seqs : (step + 1) * seqs]
 
     stages = (reduce_0, reduce_1, reduce_2, reduce_3, reduce_4)
     for t in range(CHUNKS + len(stages) - 1):
@@ -442,10 +450,12 @@
     rows = DEVICES * ROWS
     return pl.pallas_call(
         layer_kernel,
-        out_shape=jax.ShapeDtypeStruct(residual.shape, BF16),
-        in_specs=[vmem] * 6 + [smem] + [vmem] * 3 + [hbm] * 3,
+        out_shape=jax.ShapeDtypeStruct(residual.shape, F32),
+        in_specs=[vmem] * 2 + [hbm] * 2 + [vmem] * 2 + [smem] + [vmem] * 3 + [hbm] * 3,
         out_specs=vmem,
         scratch_shapes=[
+            pltpu.VMEM(key_cache.shape, BF16),
+            pltpu.VMEM(value_cache.shape, BF16),
             pltpu.VMEM((CHUNKS, local, units, cols), BF16),
             pltpu.VMEM((CHUNKS, local, units, cols), BF16),
             pltpu.VMEM((CHUNKS, local, units, cols), BF16),
@@ -466,7 +476,7 @@
             pltpu.VMEM((CHUNKS, 2, 4, ROWS, cols), BF16),
             pltpu.VMEM((CHUNKS, 4, ROWS, cols), BF16),
             pltpu.VMEM((CHUNKS, 4, ROWS, cols), BF16),
-            pltpu.SemaphoreType.DMA((3, CHUNKS)),
+            pltpu.SemaphoreType.DMA((4, CHUNKS)),
             pltpu.SemaphoreType.DMA((CHUNKS + 1, 11)),
             pltpu.SemaphoreType.DMA((CHUNKS + 1, 11)),
             pltpu.SemaphoreType.DMA((CHUNKS, 10)),
@@ -479,7 +489,7 @@
         residual, queries, key_cache, value_cache, new_keys, new_values, cache_len,
         norm_gain, expert_ids, gate_scores, gate_weight, up_weight,
         down_weight,
-    )
+    ).astype(BF16)
 
 
 def solution(mesh):

time: 53 us -> 54 us (1.019)
  other arithmetic: 0 us -> 1.55 us
  local copies, waits for them, and re-layouts: 1.45 us -> 0 us
  Pallas kernels: 51.4 us -> 52.2 us
    convert_element_type x0 -> x1, other arithmetic: none -> 1.55 us  [per_device_kernel(): return pl.pallas_call(layer_kernel, out_shape=jax.ShapeDtypeStruct(residu...]
    unnamed x1 -> x0, local copies, waits for them, and re-layouts: 1.45 us -> none
    pallas_call x1, Pallas kernels: 51.4 us -> 52.2 us  [per_device_kernel(): pl.pallas_call(layer_kernel, out_shape=jax.ShapeDtypeStruct(residual.shap...]
where the time goes in v3:
time: 54 us; the launch traced here: 53.8 us
  Pallas kernels  52.2 us (97%)
  other arithmetic  1.55 us (3%)
    pallas_call x1, Pallas kernels, per_device_kernel(): pl.pallas_call(layer_kernel, out_shape=jax.ShapeDtypeStruct(residual.shap...  52.2 us
    convert_element_type x1, other arithmetic, per_device_kernel(): return pl.pallas_call(layer_kernel, out_shape=jax.ShapeDtypeStruct(residu...  1.55 us

profile of v3, /device:TPU:0, one launch (start us, length us, event | category | flops | bytes accessed | tf_op | source)
XLA Modules:
  0.0 53.8 jit_solution(5392972089496736092)
XLA Ops:
  0.0 52.2 %shard_map.127 = f32[3,2,4096]{2,1,0:T(2,128)} custom-call(bf16[3,2,4096]{2,1,0:T(2,128)(2,1)} %res_ref.1, bf16[3,2,4096]{2,1,0:T(2,128)(2,1)} %q_ref.1, bf16[2,1024,256]{2,1,0:T(8,128)(2,1)} %k_hbm.1, bf16[2,1024,256]{2,1,0:T(8,128)(2,1)} %v_hbm.1, bf16[3,2,256]{2,1,0:T(2,128)(2,1)} %nk_ref.1, bf16[3,2,256]{2,1,0:T(2,128)(2,1)} %nv_ref.1, s32[2]{0:T(128)} %len_ref.1, ...), custom_call_target="tpu_custom_call" | custom-call | tf_op jit(solution)/shard_map/pallas_call | solution.py:451
  52.2 1.5 %convert_element_type.3 = bf16[3,2,4096]{2,1,0:T(2,128)(2,1)} convert(f32[3,2,4096]{2,1,0:T(2,128)} %shard_map.127) | non-fusion elementwise | flops 24576 | bytes 147456 | tf_op jit(solution)/shard_map/convert_element_type | solution.py:492
